TPU v7x, 32 devices: a whole 2x2x4 slice. The times are simulated.
32 devices in a mesh: row: 4 (over x, core), col: 8 (over z, y).
Axes of the slice: x: 2, y: 2, z: 4, core: 2. Of those that a mesh axis runs over, the one named last changes fastest.
Arguments:
- features: bfloat16 [32768, 256], P(('row', 'col')), may hold values from -6 to 6
- weight: bfloat16 [256, 256], replicated, may hold values from -0.375 to 0.375
- layer_bias: float32 [256], replicated, may hold values from -3 to 3
- adj_tiles: bfloat16 [1536, 128, 128], P(('row', 'col')), may hold values from 0 to 0.079589844
- tile_source: int32 [1536], P(('row', 'col')), may hold values from 0 to 11, as said below
- tile_target: int32 [1536], P(('row', 'col')), may hold values from 0 to 23, as said below
- tile_count: int32 [32], P(('row', 'col')), may hold values from 1 to 48, as said below
- fetch_list: int32 [128, 3], P(('row', 'col')), may hold values from -1 to 7, as said below
- deliver_list: int32 [256, 3], P(('row', 'col')), may hold values from -1 to 7, as said below
- cotangent: bfloat16 [32768, 256], P(('row', 'col')), may hold values from -6 to 6
Outputs:
- layer_out: bfloat16 [32768, 256], P(('row', 'col'))
- grad_features: bfloat16 [32768, 256], P(('row', 'col'))
- grad_weight: float32 [256, 256], replicated
- grad_bias: float32 [256], replicated
Inputs may be any that keep to these rules, and one draw needn't show every extreme that they name: `tile_source`: each entry names a source slot q * 3 + j of its device whose fetch_list entry is not -1. `tile_target`: each entry names a row slot p * 3 + j of its device whose deliver_list entry is not -1. `tile_count`: live tiles are the first ones of a device; in every draw some device has 48 live tiles. `fetch_list`: each list holds one or more distinct local block numbers, then -1 in its unused slots; in every draw some device has all its lists full. `deliver_list`: each list holds one or more distinct local block numbers, then -1 in its unused slots; in every draw some owner has all its lists full.
All inputs are finite; a program needn't handle non-finite values.
Results may differ from a plain program's by a relative error of at most 0.0085.
Values may be sent and summed in bfloat16 or wider, within the bound.
A program may use at most 128 MiB of HBM per device.

v0:
```python
import math

import jax
import jax.numpy as jnp
from jax import lax
from jax.sharding import PartitionSpec as P


def silu_grad(values):
    logistic = jax.nn.sigmoid(values)
    return logistic * (1.0 + values * (1.0 - logistic))


def tile_sums(adj_tiles, operand, take_slot, put_slot, live_count, slot_total, transpose):
    pattern = "kji,kjf->kif" if transpose else "kij,kjf->kif"
    tile_total = adj_tiles.shape[0]
    live_mask = jnp.arange(tile_total, dtype=jnp.int32) < live_count
    products = jnp.einsum(
        pattern, adj_tiles, operand[take_slot], preferred_element_type=jnp.float32
    )
    products = jnp.where(live_mask[:, None, None], products, 0.0)
    return jax.ops.segment_sum(products, put_slot, num_segments=slot_total)


def body(
    features,
    weight,
    layer_bias,
    adj_tiles,
    tile_source,
    tile_target,
    tile_count,
    fetch_list,
    deliver_list,
    cotangent,
):
    row_devices = lax.axis_size("row")
    col_devices = lax.axis_size("col")
    node_rows, feat_width = features.shape
    tile_side = adj_tiles.shape[1]
    own_blocks = node_rows // tile_side
    fetch_cap = fetch_list.shape[1]
    deliver_cap = deliver_list.shape[1]
    block_cells = tile_side * feat_width
    live_count = tile_count[0]
    projected = jnp.dot(features, weight, preferred_element_type=jnp.float32).astype(jnp.bfloat16)
    column = lax.all_gather(projected, "row", axis=0, tiled=True)
    source_operand = column.reshape(row_devices * own_blocks, tile_side, feat_width)
    global_ids = (
        jnp.arange(row_devices, dtype=jnp.int32)[:, None] * own_blocks + jnp.maximum(fetch_list, 0)
    ).reshape(-1)
    take_src = global_ids[tile_source]
    row_sums = tile_sums(
        adj_tiles,
        source_operand,
        take_src,
        tile_target,
        live_count,
        col_devices * deliver_cap,
        False,
    )
    outgoing_rows = row_sums.astype(jnp.bfloat16).reshape(col_devices, deliver_cap, block_cells)
    incoming = lax.all_to_all(outgoing_rows, "col", split_axis=0, concat_axis=0, tiled=True)
    deliver_hot = (
        deliver_list.reshape(-1)[None, :] == jnp.arange(own_blocks, dtype=jnp.int32)[:, None]
    ).astype(jnp.bfloat16)
    aggregated = jnp.dot(
        deliver_hot,
        incoming.reshape(col_devices * deliver_cap, block_cells),
        preferred_element_type=jnp.float32,
    )
    pre_act = aggregated.reshape(node_rows, feat_width) + layer_bias
    layer_out = jax.nn.silu(pre_act).astype(jnp.bfloat16)
    slopes = cotangent.astype(jnp.float32) * silu_grad(pre_act)
    bias_term = jnp.sum(slopes, axis=0)
    slope_blocks = slopes.astype(jnp.bfloat16).reshape(own_blocks, tile_side, feat_width)
    wanted_rows = slope_blocks[jnp.maximum(deliver_list, 0).reshape(-1)].reshape(
        col_devices, deliver_cap, tile_side, feat_width
    )
    row_values = lax.all_to_all(
        wanted_rows, "col", split_axis=0, concat_axis=0, tiled=True
    ).reshape(col_devices * deliver_cap, tile_side, feat_width)
    src_sums = tile_sums(
        adj_tiles, row_values, tile_target, tile_source, live_count, row_devices * fetch_cap, True
    )
    rounded = src_sums.astype(jnp.bfloat16).reshape(row_devices * fetch_cap, block_cells)
    valid_slots = fetch_list.reshape(-1) >= 0
    onehot = (
        (global_ids[None, :] == jnp.arange(row_devices * own_blocks, dtype=jnp.int32)[:, None])
        & valid_slots[None, :]
    ).astype(jnp.bfloat16)
    dense_rows = jnp.dot(onehot, rounded, preferred_element_type=jnp.float32)
    owned_sums = lax.psum_scatter(
        dense_rows.astype(jnp.bfloat16), "row", scatter_dimension=0, tiled=True
    ).astype(jnp.float32)
    grad_proj = owned_sums.reshape(node_rows, feat_width).astype(jnp.bfloat16)
    grad_features = jnp.dot(grad_proj, weight.T, preferred_element_type=jnp.float32).astype(
        jnp.bfloat16
    )
    weight_term = lax.dot_general(
        features, grad_proj, (((0,), (0,)), ((), ())), preferred_element_type=jnp.float32
    )
    grad_weight, grad_bias = lax.psum((weight_term, bias_term), ("row", "col"))
    grad_scale = 1.0 / math.sqrt(node_rows * row_devices * col_devices)
    return (layer_out, grad_features, grad_weight * grad_scale, grad_bias * grad_scale)


def solution(mesh):
    return jax.shard_map(
        body,
        mesh=mesh,
        in_specs=(
            P(("row", "col"), None),
            P(),
            P(),
            P(("row", "col"), None, None),
            P(("row", "col")),
            P(("row", "col")),
            P(("row", "col")),
            P(("row", "col"), None),
            P(("row", "col"), None),
            P(("row", "col"), None),
        ),
        out_specs=(P(("row", "col"), None), P(("row", "col"), None), P(), P()),
        check_vma=False,
    )
```

profile of v0, /device:TPU:0, one launch (start us, length us, event | category | flops | bytes accessed | tf_op | source)
XLA Modules:
  0.0 380.0 jit_solution(9277244789224920777)
XLA Ops:
  7.2 2.3 convolution_convert_fusion.2
  9.5 0.8 maximum_add_fusion
  11.7 0.8 gather_fusion
  12.5 23.0 %all-gather.2.cloned.1.call-done = bf16[4096,256]{1,0:T(8,128)(2,1)} async-done(((bf16[1024,256]{1,0:T(8,128)(2,1)}), bf16[4096,256]{1,0:T(8,128)(2,1)}) %all-gather.2.cloned.1.call-update) | async-done | bytes 2097168 | tf_op jit(solution)/shard_map/all_gather | solution.py:47
  35.5 4.1 %gather_fusion.1 = bf16[48,128,256]{2,1,0:T(8,128)(2,1)} fusion(bf16[32,128,256]{2,1,0:T(8,128)(2,1)} %bitcast.36, s32[1024]{0:T(1024)S(1)} %pad_clamp_fusion.2), kind=kCustom, calls=%fused_computation.1 | custom fusion | bytes 6291648 | tf_op jit(solution)/shard_map/gather | solution.py:19
  39.6 5.9 %select_bitcast_fusion.1 = f32[48,128,256]{1,2,0:T(8,128)} fusion(pred[48]{0:T(512)(128)(4,1)S(1)} %iota_compare_fusion.3, bf16[48,128,256]{2,1,0:T(8,128)(2,1)} %gather_fusion.1, bf16[48,128,128]{2,1,0:T(8,128)(2,1)S(1)} %copy-done), kind=kOutput, calls=%fused_computation.8 | convolution fusion | flops 404226048 | bytes 11010096 | tf_op jit(solution)/shard_map/kij,kjf->kif/dot_general | solution.py:18
  45.5 6.6 %copy.21 = f32[48,128,256]{2,1,0:T(8,128)} copy(f32[48,128,256]{1,2,0:T(8,128)} %select_bitcast_fusion.1) | data formatting | bytes 12582912 | tf_op jit(solution)/shard_map/jit(_where)/select_n | solution.py:21
  52.0 2.0 broadcast_in_dim.43
  54.1 14.5 %scatter_fusion = f32[24,128,256]{2,1,0:T(8,128)} fusion(f32[24,128,256]{2,1,0:T(8,128)} %broadcast_in_dim.43, s32[48]{0:T(128)S(1)} %copy-done.6, f32[48,128,256]{2,1,0:T(8,128)} %copy.21), kind=kCustom, calls=%fused_computation.4 | custom fusion | flops 1572864 | bytes 18874560 | tf_op jit(solution)/shard_map/scatter-add | solution.py:22
  68.6 2.1 convert_element_type.32
  70.7 2.1 reshape.103
  72.8 5.1 %all-to-all-start = ((bf16[8,3,32768]{2,1,0:T(4,128)(2,1)}), bf16[8,3,32768]{2,1,0:T(4,128)(2,1)}, u32[]{:S(2)}, u32[]{:S(2)}) async-start(bf16[8,3,32768]{2,1,0:T(4,128)(2,1)} %reshape.103), calls=%async_computation | async-start | bytes 4194304 | tf_op jit(solution)/shard_map/all_to_all | solution.py:63
  78.3 48.7 %all-to-all-done = bf16[8,3,32768]{2,1,0:T(4,128)(2,1)} async-done(((bf16[8,3,32768]{2,1,0:T(4,128)(2,1)}), bf16[8,3,32768]{2,1,0:T(4,128)(2,1)}, u32[]{:S(2)}, u32[]{:S(2)}) %all-to-all-start) | async-done | bytes 1572896 | tf_op jit(solution)/shard_map/all_to_all | solution.py:63
  127.0 2.9 reshape.104
  129.9 1.4 fusion.4
  131.4 1.4 reshape.105
  132.8 2.4 fusion.8
  135.1 1.9 gather_fusion.2
  137.0 3.6 all-to-all-start.1
  141.0 36.9 %all-to-all-done.1 = bf16[8,3,128,256]{3,2,1,0:T(8,128)(2,1)S(1)} async-done(((bf16[8,3,128,256]{3,2,1,0:T(8,128)(2,1)}), bf16[8,3,128,256]{3,2,1,0:T(8,128)(2,1)S(1)}, u32[]{:S(2)}, u32[]{:S(2)}) %all-to-all-start.1) | async-done | bytes 1572896 | tf_op jit(solution)/shard_map/all_to_all | solution.py:80
  177.8 2.5 gather_fusion.3
  180.4 5.9 %select_bitcast_fusion = f32[48,128,256]{1,2,0:T(8,128)} fusion(pred[48]{0:T(512)(128)(4,1)S(1)} %iota_compare_fusion.3, bf16[48,128,256]{2,1,0:T(8,128)(2,1)} %gather_fusion.3, bf16[48,128,128]{2,1,0:T(8,128)(2,1)S(1)} %copy-done), kind=kOutput, calls=%fused_computation.7 | convolution fusion | flops 404226048 | bytes 11010096 | tf_op jit(solution)/shard_map/kji,kjf->kif/dot_general | solution.py:18
  186.3 6.5 %copy.24 = f32[48,128,256]{2,1,0:T(8,128)} copy(f32[48,128,256]{1,2,0:T(8,128)} %select_bitcast_fusion) | data formatting | bytes 12582912 | tf_op jit(solution)/shard_map/jit(_where)/select_n | solution.py:21
  193.0 9.4 %scatter_fusion.1 = f32[12,128,256]{2,1,0:T(8,128)S(1)} fusion(f32[12,128,256]{2,1,0:T(8,128)S(1)} %broadcast_in_dim.48, s32[48]{0:T(128)S(1)} %copy-done.7, f32[48,128,256]{2,1,0:T(8,128)} %copy.24), kind=kCustom, calls=%fused_computation.5 | custom fusion | flops 1572864 | bytes 18874560 | tf_op jit(solution)/shard_map/scatter-add | solution.py:22
  203.2 2.0 convolution_convert_fusion
  205.3 37.6 %psum.15 = f32[256]{0:T(256)S(1)} all-reduce(f32[256]{0:T(256)S(1)} %get-tuple-element.12), channel_id=1, replica_groups=mesh['row'=4,'col'=8] {'row','col'}, use_global_device_ids=true, to_apply=%region_5.6 | all-reduce | flops 256 | bytes 2048 | tf_op jit(solution)/shard_map/psum | solution.py:103
  243.4 1.3 convert_element_type.38
  244.7 1.0 convolution_bitcast_fusion
  245.8 1.1 convolution_convert_fusion.1
  247.0 124.7 %all-reduce.2.cloned.1.call-done = f32[256,256]{0,1:T(8,128)} async-done(((f32[256,256]{0,1:T(8,128)}), f32[256,256]{0,1:T(8,128)}) %all-reduce.2.cloned.1.call-update) | async-done | bytes 262160 | tf_op jit(solution)/shard_map/psum | solution.py:103
  371.6 1.0 broadcast_multiply_fusion
  372.6 0.8 copy.25
  (46 shorter events, 3.1 us)
Async XLA Ops:
  7.2 32.4 %copy-start = (bf16[48,128,128]{2,1,0:T(8,128)(2,1)S(1)}, bf16[48,128,128]{2,1,0:T(8,128)(2,1)}, u32[]{:S(2)}) copy-start(bf16[48,128,128]{2,1,0:T(8,128)(2,1)} %param.13) | copy-start | bytes 4718596
  7.2 28.3 %all-gather.2.cloned.1.call-start = ((), (), s32[]{:S(2)}) async-start(), calls=%async_computation.3 | async-start | bytes 2621440 | tf_op jit(solution)/shard_map/all_gather | solution.py:47
  52.0 2.1 copy-start.6
  70.7 7.3 %copy-start.3 = (s32[8,3]{0,1:T(4,128)S(1)}, s32[8,3]{0,1:T(4,128)}, u32[]{:S(2)}) copy-start(s32[8,3]{0,1:T(4,128)} %param.18) | copy-start | bytes 292
  72.8 54.2 %all-to-all-start = ((bf16[8,3,32768]{2,1,0:T(4,128)(2,1)}), bf16[8,3,32768]{2,1,0:T(4,128)(2,1)}, u32[]{:S(2)}, u32[]{:S(2)}) async-start(bf16[8,3,32768]{2,1,0:T(4,128)(2,1)} %reshape.103), calls=%async_computation | async-start | bytes 4194304 | tf_op jit(solution)/shard_map/all_to_all | solution.py:63
  129.9 2.8 copy-start.5
  135.1 5.7 %copy-start.4 = (s32[4,3]{1,0:T(4,128)S(1)}, s32[4,3]{1,0:T(4,128)}, u32[]{:S(2)}) copy-start(s32[4,3]{1,0:T(4,128)} %param.17) | copy-start | bytes 148
  137.0 40.9 %all-to-all-start.1 = ((bf16[8,3,128,256]{3,2,1,0:T(8,128)(2,1)}), bf16[8,3,128,256]{3,2,1,0:T(8,128)(2,1)S(1)}, u32[]{:S(2)}, u32[]{:S(2)}) async-start(bf16[8,3,128,256]{3,2,1,0:T(8,128)(2,1)} %bitcast.35), calls=%async_computation.1 | async-start | bytes 3145728 | tf_op jit(solution)/shard_map/all_to_all | solution.py:80
  140.6 102.8 %reduce-scatter.2.cloned.1.call-start = ((), (), s32[]{:S(2)}) async-start(), calls=%async_computation.4 | async-start | bytes 2621440 | tf_op jit(solution)/shard_map/reduce_scatter | solution.py:93
  186.3 6.7 %copy-start.7 = (s32[48]{0:T(128)S(1)}, s32[48]{0:T(128)}, u32[]{:S(2)}) copy-start(s32[48]{0:T(128)} %param.14) | copy-start | bytes 580
  203.2 41.6 %copy-start.1 = (bf16[1024,256]{1,0:T(8,128)(2,1)S(1)}, bf16[1024,256]{1,0:T(8,128)(2,1)}, u32[]{:S(2)}) copy-start(bf16[1024,256]{1,0:T(8,128)(2,1)} %param.10) | copy-start | bytes 1572868
  205.2 40.6 %copy-start.2 = (bf16[256,256]{1,0:T(8,128)(2,1)S(1)}, bf16[256,256]{1,0:T(8,128)(2,1)}, u32[]{:S(2)}) copy-start(bf16[256,256]{1,0:T(8,128)(2,1)} %param.11) | copy-start | bytes 393220
  205.2 166.4 %all-reduce.2.cloned.1.call-start = ((), (), s32[]{:S(2)}) async-start(), calls=%async_computation.5 | async-start | bytes 524288 | tf_op jit(solution)/shard_map/psum | solution.py:103
Sparse Core Ops, SparseCore 0:
  10.1 25.2 all-gather.1
  205.3 29.6 reduce-scatter.1
  245.9 125.6 all-reduce.1
where the time goes:
time: 381 us; the launch traced here: 380 us
  waiting for transfers between devices  233 us (61%)
  blocking collectives  37.6 us (10%)
  local copies, waits for them, and re-layouts  34.3 us (9%)
  other arithmetic  31.5 us (8%)
  matrix products  19.7 us (5%)
  between operations  14.6 us (4%)
  starting transfers between devices  9.06 us (2%)
    psum x1, waiting for transfers between devices, body(): grad_weight, grad_bias = lax.psum((weight_term, bias_term), ('row', 'col'))  125 us
    all_to_all x1, waiting for transfers between devices, body(): lax.all_to_all(outgoing_rows, 'col', split_axis=0, concat_axis=0, tiled=T...  48.7 us
    psum x1, blocking collectives, body(): grad_weight, grad_bias = lax.psum((weight_term, bias_term), ('row', 'col'))  37.6 us
    all_to_all x1, waiting for transfers between devices, body(): lax.all_to_all(wanted_rows, 'col', split_axis=0, concat_axis=0, tiled=True)  36.9 us
    scatter-add x2, other arithmetic, tile_sums(): return jax.ops.segment_sum(products, put_slot, num_segments=slot_total)  23.9 us
    all_gather x1, waiting for transfers between devices, body(): column = lax.all_gather(projected, 'row', axis=0, tiled=True)  23 us
    select_n x2, local copies, waits for them, and re-layouts, tile_sums(): products = jnp.where(live_mask[:, None, None], products, 0.0)  13.1 us
    dot_general x2, matrix products, tile_sums(): jnp.einsum(pattern, adj_tiles, operand[take_slot], preferred_element_type...  11.8 us
  transfers between devices with their start and end apart: 5, of which 4 were waited for; matrix products, arithmetic and copies ran while one was open for 1% of the time, Pallas kernels for 0%

commit v1 on v0

v1 whole, which is shorter than its diff:
```python
import functools
import math

import jax
import jax.numpy as jnp
from jax import lax
from jax.experimental import pallas as pl
from jax.experimental.pallas import tpu as pltpu
from jax.sharding import PartitionSpec as P

F32 = jnp.float32
BF16 = jnp.bfloat16
HALVES = 2


def loop(lower, upper, step):
    def run(i, carry):
        step(i)
        return carry

    lax.fori_loop(lower, upper, run, 0)


def layer_kernel(
    R,
    C,
    fuse_sum,
    scale,
    take_src,
    take_row,
    prev_row,
    last_row,
    prev_src,
    last_src,
    deliver,
    features,
    weight,
    bias,
    tiles,
    lists,
    cotangent,
    layer_out,
    grad_features,
    grad_weight,
    grad_bias,
    *scratch,
):
    H = HALVES
    scratch = list(scratch)

    def take(count):
        taken = scratch[:count]
        del scratch[:count]
        return taken

    (list_all, proj, fetch_out, prod, turned, agg, proj_grad) = take(7)
    src = take(H)
    rows_out = take(H)
    rows_in = take(H)
    slope = take(H)
    slope_out = take(H)
    row_vals = take(H)
    back_out = take(H)
    back_in = take(H)
    (term, bias_acc, bias_row, bias_in1, bias_mid, bias_in2) = take(6)
    (part_in, part_sum, piece_in, piece_sum, piece_all, part_all) = take(6)
    (list_s, list_r, fetch_s, fetch_r, rows_s, rows_r) = take(6)
    (slope_s, slope_r, back_s, back_r, b1_s, b1_r, b2_s, b2_r) = take(8)
    (p1_s, p1_r, p2_s, p2_r, p3_s, p3_r, p4_s, p4_r) = take(8)

    r = lax.axis_index("row")
    c = lax.axis_index("col")
    T = tiles.shape[0]
    side = tiles.shape[1]
    B = proj.shape[1]
    FC = proj.shape[3]
    CF = fetch_out.shape[2]
    CO = rows_out[0].shape[1]

    def row_copy(source, target, send, recv, q):
        return pltpu.make_async_remote_copy(
            source, target, send, recv, device_id={"row": q}, device_id_type=pl.DeviceIdType.MESH
        )

    def col_copy(source, target, send, recv, p):
        return pltpu.make_async_remote_copy(
            source, target, send, recv, device_id={"col": p}, device_id_type=pl.DeviceIdType.MESH
        )

    def row_peers(step):
        loop(1, R, lambda i: step(lax.rem(r + i, R)))

    def col_peers(step):
        loop(1, C, lambda i: step(lax.rem(c + i, C)))

    barrier = pltpu.get_barrier_semaphore()
    row_peers(
        lambda q: pl.semaphore_signal(
            barrier, inc=1, device_id={"row": q}, device_id_type=pl.DeviceIdType.MESH
        )
    )
    col_peers(
        lambda p: pl.semaphore_signal(
            barrier, inc=1, device_id={"col": p}, device_id_type=pl.DeviceIdType.MESH
        )
    )
    pl.semaphore_wait(barrier, R + C - 2)

    row_peers(
        lambda q: row_copy(
            lists.at[q], list_all.at[r], list_s.at[q], list_r.at[r], q
        ).start()
    )
    list_all[r] = lists[r]

    def project(b):
        rows = pl.ds(pl.multiple_of(b * side, side), side)
        whole = jnp.dot(features[rows, :], weight[...], preferred_element_type=F32).astype(BF16)
        for h in range(H):
            proj[h, b] = whole[:, h * FC : (h + 1) * FC]

    loop(0, B, project)
    row_peers(
        lambda q: row_copy(
            lists.at[q], list_all.at[q], list_s.at[q], list_r.at[q], q
        ).wait_recv()
    )

    def picked(h, q, j):
        wanted = list_all[q, j : j + 1, :FC]
        total = jnp.zeros((side, FC), F32)
        for b in range(B):
            total = total + (wanted == b).astype(F32) * proj[h, b].astype(F32)
        return total.astype(BF16)

    def fetch_copy(h, q, frm):
        return row_copy(
            fetch_out.at[h, q], src[h].at[frm], fetch_s.at[h, q], fetch_r.at[h, frm], q
        )

    for h in range(H):

        def send_fetch(q, h=h):
            for j in range(CF):
                fetch_out[h, q, j] = picked(h, q, j)
            fetch_copy(h, q, r).start()

        row_peers(send_fetch)
        for j in range(CF):
            src[h][r, j] = picked(h, r, j)

    prod[T] = jnp.zeros((side, FC), F32)

    def clear(b):
        for h in range(H):
            agg[h, b] = jnp.zeros((side, FC), F32)

    loop(0, B, clear)

    group = math.gcd(T, 8)

    def tile_sums(left, right, index, cap, prev):
        def multiply(g):
            for u in range(group):
                k = g * group + u
                slot = index[k]
                prod[k] = jnp.dot(
                    left[k], right[slot // cap, lax.rem(slot, cap)], preferred_element_type=F32
                )

        loop(0, T // group, multiply)

        def chain(k):
            prod[k] = prod[k] + prod[prev[k]]

        loop(0, T, chain)

    def rows_copy(h, p, frm):
        return col_copy(
            rows_out[h].at[p], rows_in[h].at[frm], rows_s.at[h, p], rows_r.at[h, frm], p
        )

    for h in range(H):
        row_peers(lambda q, h=h: fetch_copy(h, q, q).wait_recv())
        tile_sums(tiles, src[h], take_src, CF, prev_row)

        def send_rows(p, h=h):
            for j in range(CO):
                rows_out[h][p, j] = prod[last_row[p * CO + j]].astype(BF16)
            rows_copy(h, p, c).start()

        col_peers(send_rows)
        for j in range(CO):
            rows_in[h][c, j] = prod[last_row[c * CO + j]].astype(BF16)

    def turn(g):
        for u in range(group):
            turned[g * group + u] = tiles[g * group + u].T

    loop(0, T // group, turn)

    strip = 16

    def add_rows(h, p):
        masks = [
            [(deliver[p * CO + j] == b).astype(F32) for j in range(CO)] for b in range(B)
        ]

        def add(i):
            rows = pl.ds(pl.multiple_of(i * strip, strip), strip)
            got = [rows_in[h][p, j, rows, :].astype(F32) for j in range(CO)]
            for b in range(B):
                total = agg[h, b, rows, :]
                for j in range(CO):
                    total = total + masks[b][j] * got[j]
                agg[h, b, rows, :] = total

        loop(0, side // strip, add)

    def slope_copy(h, p, frm):
        return col_copy(
            slope_out[h].at[p], row_vals[h].at[frm], slope_s.at[h, p], slope_r.at[h, frm], p
        )

    bias_acc[...] = jnp.zeros_like(bias_acc)
    for h in range(H):
        cols = slice(h * FC, (h + 1) * FC)
        add_rows(h, c)

        def arrive(p, h=h):
            rows_copy(h, p, p).wait_recv()
            add_rows(h, p)

        col_peers(arrive)

        def activate(b, h=h, cols=cols):
            rows = pl.ds(pl.multiple_of(b * side, side), side)
            value = agg[h, b] + bias[0:1, cols]
            logistic = 1.0 / (1.0 + jnp.exp(-value))
            layer_out[rows, cols] = (value * logistic).astype(BF16)
            grad = cotangent[rows, cols].astype(F32) * (
                logistic * (1.0 + value * (1.0 - logistic))
            )
            slope[h][b] = grad.astype(BF16)
            bias_acc[:, cols] = bias_acc[:, cols] + jnp.sum(
                grad.reshape(side // 8, 8, FC), axis=0
            )

        loop(0, B, activate)

        def send_slope(p, h=h):
            for j in range(CO):
                slope_out[h][p, j] = slope[h][jnp.maximum(deliver[p * CO + j], 0)]
            slope_copy(h, p, c).start()

        col_peers(send_slope)
        for j in range(CO):
            row_vals[h][c, j] = slope[h][jnp.maximum(deliver[c * CO + j], 0)]

    bias_row[...] = bias_acc[...]

    def bias1(q, frm):
        return row_copy(bias_row, bias_in1.at[frm], b1_s.at[q], b1_r.at[frm], q)

    def bias2(p, frm):
        return col_copy(bias_mid, bias_in2.at[frm], b2_s.at[p], b2_r.at[frm], p)

    row_peers(lambda q: bias1(q, r).start())
    bias_in1[r] = bias_acc[...]

    def back_copy(h, q, frm):
        return row_copy(
            back_out[h].at[q], back_in[h].at[frm], back_s.at[h, q], back_r.at[h, frm], q
        )

    for h in range(H):
        col_peers(lambda p, h=h: slope_copy(h, p, p).wait_recv())
        tile_sums(turned, row_vals[h], take_row, CO, prev_src)

        def send_back(q, h=h):
            for j in range(CF):
                back_out[h][q, j] = prod[last_src[q * CF + j]].astype(BF16)
            back_copy(h, q, r).start()

        row_peers(send_back)
        for j in range(CF):
            back_in[h][r, j] = prod[last_src[r * CF + j]].astype(BF16)
        if h == 0:
            row_peers(lambda q: bias1(q, q).wait_recv())
            bias_mid[...] = jnp.sum(bias_in1[...], axis=0)
            col_peers(lambda p: bias2(p, c).start())
            bias_in2[c] = bias_mid[...]

    for h in range(H):
        cols = slice(h * FC, (h + 1) * FC)
        row_peers(lambda q, h=h: back_copy(h, q, q).wait_recv())

        def gather_back(b, h=h, cols=cols):
            total = jnp.zeros((side, FC), F32)
            for q in range(R):
                for j in range(CF):
                    mask = (list_all[q, j : j + 1, :FC] == b).astype(F32)
                    total = total + mask * back_in[h][q, j].astype(F32)
            rows = pl.ds(pl.multiple_of(b * side, side), side)
            proj_grad[rows, cols] = total.astype(BF16)

        loop(0, B, gather_back)

    term[...] = lax.dot_general(
        features[...], proj_grad[...], (((0,), (0,)), ((), ())), preferred_element_type=F32
    )

    F = weight.shape[0]
    half = F // R
    piece = half // C

    def part1(q, frm):
        place = pl.ds(pl.multiple_of(q * half, 8), half)
        return row_copy(term.at[place, :], part_in.at[frm], p1_s.at[q], p1_r.at[frm], q)

    def part2(p, frm):
        place = pl.ds(pl.multiple_of(p * piece, 8), piece)
        return col_copy(part_sum.at[place, :], piece_in.at[frm], p2_s.at[p], p2_r.at[frm], p)

    def part3(p, frm):
        return col_copy(piece_sum, piece_all.at[frm], p3_s.at[p], p3_r.at[frm], p)

    def part4(q, frm):
        return row_copy(piece_all, part_all.at[frm], p4_s.at[q], p4_r.at[frm], q)

    if fuse_sum:
        row_peers(lambda q: part1(q, r).start())
        part_in[r] = term[pl.ds(pl.multiple_of(r * half, 8), half), :]

    def features_back(b):
        rows = pl.ds(pl.multiple_of(b * side, side), side)
        grad_features[rows, :] = lax.dot_general(
            proj_grad[rows, :], weight[...], (((1,), (1,)), ((), ())), preferred_element_type=F32
        ).astype(BF16)

    loop(0, B, features_back)
    col_peers(lambda p: bias2(p, p).wait_recv())
    grad_bias[...] = jnp.broadcast_to(
        jnp.sum(jnp.sum(bias_in2[...], axis=0), axis=0, keepdims=True) * scale, grad_bias.shape
    )

    if fuse_sum:
        row_peers(lambda q: part1(q, q).wait_recv())
        part_sum[...] = jnp.sum(part_in[...], axis=0)
        col_peers(lambda p: part2(p, c).start())
        piece_in[c] = part_sum[pl.ds(pl.multiple_of(c * piece, 8), piece), :]
        col_peers(lambda p: part2(p, p).wait_recv())
        piece_sum[...] = jnp.sum(piece_in[...], axis=0) * scale
        col_peers(lambda p: part3(p, c).start())
        piece_all[c] = piece_sum[...]
        col_peers(lambda p: part3(p, p).wait_recv())
        row_peers(lambda q: part4(q, r).start())
        part_all[r] = piece_all[...]
        row_peers(lambda q: part4(q, q).wait_recv())
        grad_weight[...] = part_all[...].reshape(F, F)
        row_peers(lambda q: part1(q, r).wait_send())
        col_peers(lambda p: part2(p, c).wait_send())
        col_peers(lambda p: part3(p, c).wait_send())
        row_peers(lambda q: part4(q, r).wait_send())
    else:
        grad_weight[...] = term[...]

    row_peers(
        lambda q: row_copy(
            lists.at[q], list_all.at[r], list_s.at[q], list_r.at[r], q
        ).wait_send()
    )
    row_peers(lambda q: bias1(q, r).wait_send())
    col_peers(lambda p: bias2(p, c).wait_send())
    for h in range(H):
        row_peers(lambda q, h=h: fetch_copy(h, q, r).wait_send())
        col_peers(lambda p, h=h: rows_copy(h, p, c).wait_send())
        col_peers(lambda p, h=h: slope_copy(h, p, c).wait_send())
        row_peers(lambda q, h=h: back_copy(h, q, r).wait_send())


def chains(slots, live, slot_total):
    tile_total = slots.shape[0]
    ids = jnp.arange(tile_total, dtype=jnp.int32)
    same = (slots[None, :] == slots[:, None]) & (ids[None, :] < ids[:, None])
    prev = jnp.max(jnp.where(same, ids[None, :], -1), axis=1)
    slot_ids = jnp.arange(slot_total, dtype=jnp.int32)
    here = (slots[None, :] == slot_ids[:, None]) & (ids[None, :] < live)
    last = jnp.max(jnp.where(here, ids[None, :], -1), axis=1)
    return (
        jnp.where(prev < 0, tile_total, prev).astype(jnp.int32),
        jnp.where(last < 0, tile_total, last).astype(jnp.int32),
    )


def body(
    features,
    weight,
    layer_bias,
    adj_tiles,
    tile_source,
    tile_target,
    tile_count,
    fetch_list,
    deliver_list,
    cotangent,
):
    R = lax.axis_size("row")
    C = lax.axis_size("col")
    H = HALVES
    N, F = features.shape
    T, side, _ = adj_tiles.shape
    B = N // side
    CF = fetch_list.shape[1]
    CO = deliver_list.shape[1]
    FC = F // H
    half = F // R
    piece = half // C
    fuse_sum = F % R == 0 and half % C == 0 and piece % 8 == 0
    scale = 1.0 / math.sqrt(N * R * C)
    live = tile_count[0]
    prev_row, last_row = chains(tile_target, live, C * CO)
    prev_src, last_src = chains(tile_source, live, R * CF)
    list_rows = -(-CF // 8) * 8
    lists = jnp.broadcast_to(
        jnp.pad(fetch_list, ((0, 0), (0, list_rows - CF)), constant_values=-1)[:, :, None],
        (R, list_rows, F),
    )
    V = pltpu.VMEM
    dma = pltpu.SemaphoreType.DMA
    small = piece if fuse_sum else 8
    scratch = [
        V((R, list_rows, F), jnp.int32),
        V((H, B, side, FC), BF16),
        V((H, R, CF, side, FC), BF16),
        V((T + 1, side, FC), F32),
        V((T, side, side), BF16),
        V((H, B, side, FC), F32),
        V((N, F), BF16),
        *[V((R, CF, side, FC), BF16)] * H,
        *[V((C, CO, side, FC), BF16)] * H,
        *[V((C, CO, side, FC), BF16)] * H,
        *[V((B, side, FC), BF16)] * H,
        *[V((C, CO, side, FC), BF16)] * H,
        *[V((C, CO, side, FC), BF16)] * H,
        *[V((R, CF, side, FC), BF16)] * H,
        *[V((R, CF, side, FC), BF16)] * H,
        V((F, F), F32),
        V((8, F), F32),
        V((8, F), F32),
        V((R, 8, F), F32),
        V((8, F), F32),
        V((C, 8, F), F32),
        V((R, half, F), F32),
        V((half, F), F32),
        V((C, small, F), F32),
        V((small, F), F32),
        V((C, small, F), F32),
        V((R, C, small, F), F32),
        *[dma((R,))] * 2,
        *[dma((H, R))] * 2,
        *[dma((H, C))] * 2,
        *[dma((H, C))] * 2,
        *[dma((H, R))] * 2,
        *[dma((R,))] * 2,
        *[dma((C,))] * 2,
        *[dma((R,))] * 2,
        *[dma((C,))] * 2,
        *[dma((C,))] * 2,
        *[dma((R,))] * 2,
    ]
    vmem = pl.BlockSpec(memory_space=pltpu.VMEM)
    smem = pl.BlockSpec(memory_space=pltpu.SMEM)
    layer_out, grad_features, grad_weight, grad_bias = pl.pallas_call(
        functools.partial(layer_kernel, R, C, fuse_sum, scale),
        out_shape=(
            jax.ShapeDtypeStruct((N, F), BF16),
            jax.ShapeDtypeStruct((N, F), BF16),
            jax.ShapeDtypeStruct((F, F), F32),
            jax.ShapeDtypeStruct((8, F), F32),
        ),
        in_specs=[smem] * 7 + [vmem] * 6,
        out_specs=(vmem,) * 4,
        scratch_shapes=scratch,
        compiler_params=pltpu.CompilerParams(
            collective_id=0, has_side_effects=True, vmem_limit_bytes=56 * 1024 * 1024
        ),
    )(
        tile_source,
        tile_target,
        prev_row,
        last_row,
        prev_src,
        last_src,
        deliver_list.reshape(-1),
        features,
        weight,
        layer_bias.reshape(1, F),
        adj_tiles,
        lists,
        cotangent,
    )
    grad_bias = grad_bias[0]
    if not fuse_sum:
        grad_weight = lax.psum(grad_weight, ("row", "col")) * scale
    return (layer_out, grad_features, grad_weight, grad_bias)


def solution(mesh):
    return jax.shard_map(
        body,
        mesh=mesh,
        in_specs=(
            P(("row", "col"), None),
            P(),
            P(),
            P(("row", "col"), None, None),
            P(("row", "col")),
            P(("row", "col")),
            P(("row", "col")),
            P(("row", "col"), None),
            P(("row", "col"), None),
            P(("row", "col"), None),
        ),
        out_specs=(P(("row", "col"), None), P(("row", "col"), None), P(), P()),
        check_vma=False,
    )
```

time: 381 us -> 131 us (0.34)
  waiting for transfers between devices: 233 us -> 0 us
  Pallas kernels: 0 us -> 115 us
  blocking collectives: 37.6 us -> 0 us
  other arithmetic: 31.5 us -> 4.95 us
  local copies, waits for them, and re-layouts: 34.3 us -> 8.53 us
  matrix products: 19.7 us -> 0 us
  between operations: 14.6 us -> 1.31 us
  starting transfers between devices: 9.06 us -> 0 us
    psum x1 -> x0, waiting for transfers between devices: 125 us -> none  [body(): grad_weight, grad_bias = lax.psum((weight_term, bias_term), ('row', 'col'))]
    pallas_call x0 -> x1, Pallas kernels: none -> 115 us  [body(): pl.pallas_call(functools.partial(layer_kernel, R, C, fuse_sum, scale), ou...]
    all_to_all x2 -> x0, waiting for transfers between devices: 85.6 us -> none  [the longest x1 48.7 us: body(): lax.all_to_all(outgoing_rows, 'col', split_axis=0, concat_axis=0, tiled=T...]
    psum x1 -> x0, blocking collectives: 37.6 us -> none  [body(): grad_weight, grad_bias = lax.psum((weight_term, bias_term), ('row', 'col'))]
    scatter-add x2 -> x0, other arithmetic: 23.9 us -> none  [tile_sums(): return jax.ops.segment_sum(products, put_slot, num_segments=slot_total)]
    all_gather x1 -> x0, waiting for transfers between devices: 23 us -> none  [body(): column = lax.all_gather(projected, 'row', axis=0, tiled=True)]
    dot_general x7 -> x0, matrix products: 19.7 us -> none  [the longest x2 11.8 us: tile_sums(): jnp.einsum(pattern, adj_tiles, operand[take_slot], preferred_element_type...]
    select_n x2 -> x0, local copies, waits for them, and re-layouts: 13.1 us -> none  [tile_sums(): products = jnp.where(live_mask[:, None, None], products, 0.0)]
  transfers between devices with their start and end apart: 5 -> 0, of which waited for: 4 -> 0; matrix products, arithmetic and copies ran while one was open for 1% -> 0% of each run, Pallas kernels for 0% -> 0%
where the time goes in v1:
time: 131 us; the launch traced here: 130 us
  Pallas kernels  115 us (88%)
  local copies, waits for them, and re-layouts  8.53 us (7%)
  other arithmetic  4.95 us (4%)
  between operations  1.31 us (1%)
    pallas_call x1, Pallas kernels, body(): pl.pallas_call(functools.partial(layer_kernel, R, C, fuse_sum, scale), ou...  115 us
    unnamed x6, local copies, waits for them, and re-layouts  5.2 us

profile of v1, /device:TPU:0, one launch (start us, length us, event | category | flops | bytes accessed | tf_op | source)
XLA Modules:
  0.0 130.2 jit_solution(16369500715254014318)
XLA Ops:
  1.3 0.8 select_reduce_fusion.3
  2.1 0.8 select_reduce_fusion.2
  2.8 0.5 compare_select_fusion.2.last_row
  3.4 0.5 compare_select_fusion.last_src
  3.9 0.9 select_reduce_fusion
  4.8 0.9 select_reduce_fusion.1
  5.7 0.5 compare_select_fusion.1
  6.2 0.7 pad.4
  6.9 0.8 copy.16
  7.7 0.7 reshape.24.deliver
  8.3 0.7 broadcast_in_dim.83.lists
  9.0 115.4 %shard_map.129 = (bf16[1024,256]{1,0:T(8,128)(2,1)}, bf16[1024,256]{1,0:T(8,128)(2,1)}, f32[256,256]{1,0:T(8,128)}, f32[8,256]{1,0:T(8,128)}) custom-call(s32[48]{0:T(128)} %take_src.1, s32[48]{0:T(128)} %take_row.1, s32[48]{0:T(128)} %get-tuple-element.13.prev_row, s32[24]{0:T(128)} %compare_select_fusion.2.last_row, s32[48]{0:T(128)} %get-tuple-element.12.prev_src, ...), custom_call_target="tpu_custom_call" | custom-call | tf_op jit(solution)/shard_map/pallas_call | solution.py:474
  124.4 0.0 copy-start
  124.5 1.3 slice.3
  125.8 1.9 %copy.21 = bf16[1024,256]{1,0:T(8,128)(2,1)} copy(bf16[1024,256]{1,0:T(8,128)(2,1)} %get-tuple-element.18) | data formatting | bytes 1048576
  127.6 1.9 %copy.22 = bf16[1024,256]{1,0:T(8,128)(2,1)} copy(bf16[1024,256]{1,0:T(8,128)(2,1)} %get-tuple-element.19) | data formatting | bytes 1048576
  129.5 0.0 copy-done
  129.5 0.7 copy.23
  (1 shorter events, 0.0 us)
Async XLA Ops:
  124.4 5.0 %copy-start = (f32[256,256]{1,0:T(8,128)S(1)}, f32[256,256]{1,0:T(8,128)}, u32[]{:S(2)}) copy-start(f32[256,256]{1,0:T(8,128)} %get-tuple-element.20) | copy-start | bytes 786436

commit v2 on v1

--- a/solution.py
+++ b/solution.py
@@ -32,14 +32,14 @@
     last_row,
     prev_src,
     last_src,
+    fetch,
     deliver,
     features,
     weight,
     bias,
-    tiles,
-    lists,
-    cotangent,
-    layer_out,
+    tiles_hbm,
+    cotangent_hbm,
+    layer_out_hbm,
     grad_features,
     grad_weight,
     grad_bias,
@@ -53,6 +53,7 @@
         del scratch[:count]
         return taken
 
+    (tiles, cotangent, layer_out, lists) = take(4)
     (list_all, proj, fetch_out, prod, turned, agg, proj_grad) = take(7)
     src = take(H)
     rows_out = take(H)
@@ -66,7 +67,7 @@
     (part_in, part_sum, piece_in, piece_sum, piece_all, part_all) = take(6)
     (list_s, list_r, fetch_s, fetch_r, rows_s, rows_r) = take(6)
     (slope_s, slope_r, back_s, back_r, b1_s, b1_r, b2_s, b2_r) = take(8)
-    (p1_s, p1_r, p2_s, p2_r, p3_s, p3_r, p4_s, p4_r) = take(8)
+    (p1_s, p1_r, p2_s, p2_r, p3_s, p3_r, p4_s, p4_r, local) = take(9)
 
     r = lax.axis_index("row")
     c = lax.axis_index("col")
@@ -104,6 +105,16 @@
             barrier, inc=1, device_id={"col": p}, device_id_type=pl.DeviceIdType.MESH
         )
     )
+    tiles_copy = pltpu.make_async_copy(tiles_hbm, tiles, local.at[0])
+    cotangent_copy = pltpu.make_async_copy(cotangent_hbm, cotangent, local.at[1])
+    out_copy = pltpu.make_async_copy(layer_out, layer_out_hbm, local.at[2])
+    tiles_copy.start()
+    cotangent_copy.start()
+    lists[...] = jnp.full(lists.shape, -1, jnp.int32)
+    for q in range(R):
+        for j in range(CF):
+            row = jnp.zeros((1, lists.shape[2]), jnp.int32) + fetch[q, j]
+            lists[q, j : j + 1, :] = row
     pl.semaphore_wait(barrier, R + C - 2)
 
     row_peers(
@@ -180,6 +191,7 @@
             rows_out[h].at[p], rows_in[h].at[frm], rows_s.at[h, p], rows_r.at[h, frm], p
         )
 
+    tiles_copy.wait()
     for h in range(H):
         row_peers(lambda q, h=h: fetch_copy(h, q, q).wait_recv())
         tile_sums(tiles, src[h], take_src, CF, prev_row)
@@ -203,7 +215,7 @@
 
     def add_rows(h, p):
         masks = [
-            [(deliver[p * CO + j] == b).astype(F32) for j in range(CO)] for b in range(B)
+            [(deliver[p, j] == b).astype(F32) for j in range(CO)] for b in range(B)
         ]
 
         def add(i):
@@ -223,6 +235,7 @@
         )
 
     bias_acc[...] = jnp.zeros_like(bias_acc)
+    cotangent_copy.wait()
     for h in range(H):
         cols = slice(h * FC, (h + 1) * FC)
         add_rows(h, c)
@@ -250,12 +263,14 @@
 
         def send_slope(p, h=h):
             for j in range(CO):
-                slope_out[h][p, j] = slope[h][jnp.maximum(deliver[p * CO + j], 0)]
+                slope_out[h][p, j] = slope[h][jnp.maximum(deliver[p, j], 0)]
             slope_copy(h, p, c).start()
 
         col_peers(send_slope)
         for j in range(CO):
-            row_vals[h][c, j] = slope[h][jnp.maximum(deliver[c * CO + j], 0)]
+            row_vals[h][c, j] = slope[h][jnp.maximum(deliver[c, j], 0)]
+
+    out_copy.start()
 
     bias_row[...] = bias_acc[...]
 
@@ -273,11 +288,68 @@
             back_out[h].at[q], back_in[h].at[frm], back_s.at[h, q], back_r.at[h, frm], q
         )
 
-    for h in range(H):
-        col_peers(lambda p, h=h: slope_copy(h, p, p).wait_recv())
+    F = weight.shape[0]
+    half = F // R
+    piece = half // C
+
+    def part1(h, q, frm):
+        place = pl.ds(pl.multiple_of(q * half, 8), half)
+        return row_copy(
+            term.at[h, place, :], part_in.at[h, frm], p1_s.at[h, q], p1_r.at[h, frm], q
+        )
+
+    def part2(h, p, frm):
+        place = pl.ds(pl.multiple_of(p * piece, 8), piece)
+        return col_copy(
+            part_sum.at[h, place, :], piece_in.at[h, frm], p2_s.at[h, p], p2_r.at[h, frm], p
+        )
+
+    def part3(h, p, frm):
+        return col_copy(piece_sum.at[h], piece_all.at[h, frm], p3_s.at[h, p], p3_r.at[h, frm], p)
+
+    def part4(h, q, frm):
+        return row_copy(piece_all.at[h], part_all.at[h, frm], p4_s.at[h, q], p4_r.at[h, frm], q)
+
+    def sum1(h):
+        if fuse_sum:
+            row_peers(lambda q: part1(h, q, r).start())
+            part_in[h, r] = term[h, pl.ds(pl.multiple_of(r * half, 8), half), :]
+
+    def sum2(h):
+        if fuse_sum:
+            row_peers(lambda q: part1(h, q, q).wait_recv())
+            part_sum[h] = jnp.sum(part_in[h], axis=0)
+            col_peers(lambda p: part2(h, p, c).start())
+            piece_in[h, c] = part_sum[h, pl.ds(pl.multiple_of(c * piece, 8), piece), :]
+
+    def sum3(h):
+        if fuse_sum:
+            col_peers(lambda p: part2(h, p, p).wait_recv())
+            piece_sum[h] = jnp.sum(piece_in[h], axis=0) * scale
+            col_peers(lambda p: part3(h, p, c).start())
+            piece_all[h, c] = piece_sum[h]
+
+    def sum4(h):
+        if fuse_sum:
+            col_peers(lambda p: part3(h, p, p).wait_recv())
+            row_peers(lambda q: part4(h, q, r).start())
+            part_all[h, r] = piece_all[h]
+
+    def sum5(h):
+        cols = slice(h * FC, (h + 1) * FC)
+        if fuse_sum:
+            row_peers(lambda q: part4(h, q, q).wait_recv())
+            grad_weight[:, cols] = part_all[h].reshape(F, FC)
+        else:
+            grad_weight[:, cols] = term[h]
+
+    def source_part(h):
+        col_peers(lambda p: slope_copy(h, p, p).wait_recv())
+        if h > 0:
+            sum2(h - 1)
         tile_sums(turned, row_vals[h], take_row, CO, prev_src)
 
-        def send_back(q, h=h):
+        def send_back(q):
             for j in range(CF):
                 back_out[h][q, j] = prod[last_src[q * CF + j]].astype(BF16)
             back_copy(h, q, r).start()
@@ -285,17 +357,12 @@
         row_peers(send_back)
         for j in range(CF):
             back_in[h][r, j] = prod[last_src[r * CF + j]].astype(BF16)
-        if h == 0:
-            row_peers(lambda q: bias1(q, q).wait_recv())
-            bias_mid[...] = jnp.sum(bias_in1[...], axis=0)
-            col_peers(lambda p: bias2(p, c).start())
-            bias_in2[c] = bias_mid[...]
-
-    for h in range(H):
+
+    def weight_part(h):
         cols = slice(h * FC, (h + 1) * FC)
-        row_peers(lambda q, h=h: back_copy(h, q, q).wait_recv())
-
-        def gather_back(b, h=h, cols=cols):
+        row_peers(lambda q: back_copy(h, q, q).wait_recv())
+
+        def gather_back(b):
             total = jnp.zeros((side, FC), F32)
             for q in range(R):
                 for j in range(CF):
@@ -305,32 +372,26 @@
             proj_grad[rows, cols] = total.astype(BF16)
 
         loop(0, B, gather_back)
-
-    term[...] = lax.dot_general(
-        features[...], proj_grad[...], (((0,), (0,)), ((), ())), preferred_element_type=F32
-    )
-
-    F = weight.shape[0]
-    half = F // R
-    piece = half // C
-
-    def part1(q, frm):
-        place = pl.ds(pl.multiple_of(q * half, 8), half)
-        return row_copy(term.at[place, :], part_in.at[frm], p1_s.at[q], p1_r.at[frm], q)
-
-    def part2(p, frm):
-        place = pl.ds(pl.multiple_of(p * piece, 8), piece)
-        return col_copy(part_sum.at[place, :], piece_in.at[frm], p2_s.at[p], p2_r.at[frm], p)
-
-    def part3(p, frm):
-        return col_copy(piece_sum, piece_all.at[frm], p3_s.at[p], p3_r.at[frm], p)
-
-    def part4(q, frm):
-        return row_copy(piece_all, part_all.at[frm], p4_s.at[q], p4_r.at[frm], q)
-
-    if fuse_sum:
-        row_peers(lambda q: part1(q, r).start())
-        part_in[r] = term[pl.ds(pl.multiple_of(r * half, 8), half), :]
+        term[h] = lax.dot_general(
+            features[...],
+            proj_grad[:, cols],
+            (((0,), (0,)), ((), ())),
+            preferred_element_type=F32,
+        )
+        sum1(h)
+
+    for h in range(H):
+        source_part(h)
+        if h == 0:
+            row_peers(lambda q: bias1(q, q).wait_recv())
+            bias_mid[...] = jnp.sum(bias_in1[...], axis=0)
+            col_peers(lambda p: bias2(p, c).start())
+            bias_in2[c] = bias_mid[...]
+        else:
+            sum3(h - 1)
+        weight_part(h)
+        if h > 0:
+            sum4(h - 1)
 
     def features_back(b):
         rows = pl.ds(pl.multiple_of(b * side, side), side)
@@ -338,32 +399,24 @@
             proj_grad[rows, :], weight[...], (((1,), (1,)), ((), ())), preferred_element_type=F32
         ).astype(BF16)
 
-    loop(0, B, features_back)
+    last = H - 1
+    loop(0, B // 2, features_back)
+    sum2(last)
+    loop(B // 2, B, features_back)
     col_peers(lambda p: bias2(p, p).wait_recv())
-    grad_bias[...] = jnp.broadcast_to(
-        jnp.sum(jnp.sum(bias_in2[...], axis=0), axis=0, keepdims=True) * scale, grad_bias.shape
-    )
-
+    grad_bias[...] = jnp.sum(jnp.sum(bias_in2[...], axis=0), axis=0, keepdims=True) * scale
+    sum3(last)
+    for h in range(last):
+        sum5(h)
+    sum4(last)
+    sum5(last)
     if fuse_sum:
-        row_peers(lambda q: part1(q, q).wait_recv())
-        part_sum[...] = jnp.sum(part_in[...], axis=0)
-        col_peers(lambda p: part2(p, c).start())
-        piece_in[c] = part_sum[pl.ds(pl.multiple_of(c * piece, 8), piece), :]
-        col_peers(lambda p: part2(p, p).wait_recv())
-        piece_sum[...] = jnp.sum(piece_in[...], axis=0) * scale
-        col_peers(lambda p: part3(p, c).start())
-        piece_all[c] = piece_sum[...]
-        col_peers(lambda p: part3(p, p).wait_recv())
-        row_peers(lambda q: part4(q, r).start())
-        part_all[r] = piece_all[...]
-        row_peers(lambda q: part4(q, q).wait_recv())
-        grad_weight[...] = part_all[...].reshape(F, F)
-        row_peers(lambda q: part1(q, r).wait_send())
-        col_peers(lambda p: part2(p, c).wait_send())
-        col_peers(lambda p: part3(p, c).wait_send())
-        row_peers(lambda q: part4(q, r).wait_send())
-    else:
-        grad_weight[...] = term[...]
+        for h in range(H):
+            row_peers(lambda q, h=h: part1(h, q, r).wait_send())
+            col_peers(lambda p, h=h: part2(h, p, c).wait_send())
+            col_peers(lambda p, h=h: part3(h, p, c).wait_send())
+            row_peers(lambda q, h=h: part4(h, q, r).wait_send())
+    out_copy.wait()
 
     row_peers(
         lambda q: row_copy(
@@ -379,18 +432,24 @@
         row_peers(lambda q, h=h: back_copy(h, q, r).wait_send())
 
 
-def chains(slots, live, slot_total):
-    tile_total = slots.shape[0]
-    ids = jnp.arange(tile_total, dtype=jnp.int32)
-    same = (slots[None, :] == slots[:, None]) & (ids[None, :] < ids[:, None])
-    prev = jnp.max(jnp.where(same, ids[None, :], -1), axis=1)
-    slot_ids = jnp.arange(slot_total, dtype=jnp.int32)
-    here = (slots[None, :] == slot_ids[:, None]) & (ids[None, :] < live)
-    last = jnp.max(jnp.where(here, ids[None, :], -1), axis=1)
-    return (
-        jnp.where(prev < 0, tile_total, prev).astype(jnp.int32),
-        jnp.where(last < 0, tile_total, last).astype(jnp.int32),
-    )
+def chain_kernel(source, target, count, prev_row, last_row, prev_src, last_src):
+    tile_total = source.shape[0]
+    live = count[0]
+    for last in (last_row, last_src):
+
+        def clear(s, last=last):
+            last[s] = tile_total
+
+        loop(0, last.shape[0], clear)
+
+    def link(k):
+        for slots, prev, last in ((target, prev_row, last_row), (source, prev_src, last_src)):
+            slot = slots[k]
+            before = last[slot]
+            prev[k] = before
+            last[slot] = jnp.where(k < live, k, before)
+
+    loop(0, tile_total, link)
 
 
 def body(
@@ -418,18 +477,26 @@
     piece = half // C
     fuse_sum = F % R == 0 and half % C == 0 and piece % 8 == 0
     scale = 1.0 / math.sqrt(N * R * C)
-    live = tile_count[0]
-    prev_row, last_row = chains(tile_target, live, C * CO)
-    prev_src, last_src = chains(tile_source, live, R * CF)
     list_rows = -(-CF // 8) * 8
-    lists = jnp.broadcast_to(
-        jnp.pad(fetch_list, ((0, 0), (0, list_rows - CF)), constant_values=-1)[:, :, None],
-        (R, list_rows, F),
-    )
+    vmem = pl.BlockSpec(memory_space=pltpu.VMEM)
+    smem = pl.BlockSpec(memory_space=pltpu.SMEM)
+    hbm = pl.BlockSpec(memory_space=pl.ANY)
+    prev_row, last_row, prev_src, last_src = pl.pallas_call(
+        chain_kernel,
+        out_shape=tuple(
+            jax.ShapeDtypeStruct((size,), jnp.int32) for size in (T, C * CO, T, R * CF)
+        ),
+        in_specs=[smem] * 3,
+        out_specs=(smem,) * 4,
+    )(tile_source, tile_target, tile_count)
     V = pltpu.VMEM
     dma = pltpu.SemaphoreType.DMA
     small = piece if fuse_sum else 8
     scratch = [
+        V((T, side, side), BF16),
+        V((N, F), BF16),
+        V((N, F), BF16),
+        V((R, list_rows, F), jnp.int32),
         V((R, list_rows, F), jnp.int32),
         V((H, B, side, FC), BF16),
         V((H, R, CF, side, FC), BF16),
@@ -445,18 +512,18 @@
         *[V((C, CO, side, FC), BF16)] * H,
         *[V((R, CF, side, FC), BF16)] * H,
         *[V((R, CF, side, FC), BF16)] * H,
-        V((F, F), F32),
+        V((H, F, FC), F32),
         V((8, F), F32),
         V((8, F), F32),
         V((R, 8, F), F32),
         V((8, F), F32),
         V((C, 8, F), F32),
-        V((R, half, F), F32),
-        V((half, F), F32),
-        V((C, small, F), F32),
-        V((small, F), F32),
-        V((C, small, F), F32),
-        V((R, C, small, F), F32),
+        V((H, R, half, FC), F32),
+        V((H, half, FC), F32),
+        V((H, C, small, FC), F32),
+        V((H, small, FC), F32),
+        V((H, C, small, FC), F32),
+        V((H, R, C, small, FC), F32),
         *[dma((R,))] * 2,
         *[dma((H, R))] * 2,
         *[dma((H, C))] * 2,
@@ -464,23 +531,22 @@
         *[dma((H, R))] * 2,
         *[dma((R,))] * 2,
         *[dma((C,))] * 2,
-        *[dma((R,))] * 2,
-        *[dma((C,))] * 2,
-        *[dma((C,))] * 2,
-        *[dma((R,))] * 2,
+        *[dma((H, R))] * 2,
+        *[dma((H, C))] * 2,
+        *[dma((H, C))] * 2,
+        *[dma((H, R))] * 2,
+        dma((3,)),
     ]
-    vmem = pl.BlockSpec(memory_space=pltpu.VMEM)
-    smem = pl.BlockSpec(memory_space=pltpu.SMEM)
     layer_out, grad_features, grad_weight, grad_bias = pl.pallas_call(
         functools.partial(layer_kernel, R, C, fuse_sum, scale),
         out_shape=(
             jax.ShapeDtypeStruct((N, F), BF16),
             jax.ShapeDtypeStruct((N, F), BF16),
             jax.ShapeDtypeStruct((F, F), F32),
-            jax.ShapeDtypeStruct((8, F), F32),
+            jax.ShapeDtypeStruct((1, F), F32),
         ),
-        in_specs=[smem] * 7 + [vmem] * 6,
-        out_specs=(vmem,) * 4,
+        in_specs=[smem] * 8 + [vmem] * 3 + [hbm] * 2,
+        out_specs=(hbm,) + (vmem,) * 3,
         scratch_shapes=scratch,
         compiler_params=pltpu.CompilerParams(
             collective_id=0, has_side_effects=True, vmem_limit_bytes=56 * 1024 * 1024
@@ -492,15 +558,15 @@
         last_row,
         prev_src,
         last_src,
-        deliver_list.reshape(-1),
+        fetch_list,
+        deliver_list,
         features,
         weight,
         layer_bias.reshape(1, F),
         adj_tiles,
-        lists,
         cotangent,
     )
-    grad_bias = grad_bias[0]
+    grad_bias = grad_bias.reshape(F)
     if not fuse_sum:
         grad_weight = lax.psum(grad_weight, ("row", "col")) * scale
     return (layer_out, grad_features, grad_weight, grad_bias)

time: 131 us -> 127 us (0.969)
  other arithmetic: 4.95 us -> 0 us
  Pallas kernels: 115 us -> 119 us
  local copies, waits for them, and re-layouts: 8.53 us -> 6.4 us
    reduce_max x4 -> x0, other arithmetic: 3.38 us -> none  [the longest x2 1.82 us: chains(): prev = jnp.max(jnp.where(same, ids[None, :], -1), axis=1)]
    pallas_call x0 -> x1, Pallas kernels: none -> 2.14 us  [body(): pl.pallas_call(chain_kernel, out_shape=tuple((jax.ShapeDtypeStruct((size,...]
    select_n x3 -> x0, other arithmetic: 1.57 us -> none  [the longest x2 1.04 us: chains(): jnp.where(last < 0, tile_total, last).astype(jnp.int32)]
    unnamed x6 -> x9, local copies, waits for them, and re-layouts: 5.2 us -> 6.4 us
where the time goes in v2:
time: 127 us
  Pallas kernels  119 us (94%)
  local copies, waits for them, and re-layouts  6.4 us (5%)
  between operations  1.31 us (1%)
    pallas_call x1, Pallas kernels, body(): pl.pallas_call(functools.partial(layer_kernel, R, C, fuse_sum, scale), ou...  117 us
    unnamed x9, local copies, waits for them, and re-layouts  6.4 us

profile of v2, /device:TPU:0, one launch (start us, length us, event | category | flops | bytes accessed | tf_op | source)
XLA Modules:
  0.0 126.5 jit_solution(16464381517972195940)
XLA Ops:
  1.3 2.1 %shard_map.129 = (s32[48]{0:T(128)}, s32[24]{0:T(128)}, s32[48]{0:T(128)}, s32[12]{0:T(128)}) custom-call(s32[48]{0:T(128)} %take_src.1, s32[48]{0:T(128)} %take_row.1, s32[1]{0:T(128)S(6)} %copy.19.count), custom_call_target="tpu_custom_call" | custom-call | tf_op jit(solution)/shard_map/pallas_call | solution.py:484
  3.4 1.4 %copy.14.deliver = s32[8,3]{1,0:T(8,128)} copy(s32[8,3]{0,1:T(4,128)} %param.18) | data formatting | bytes 192 | tf_op args[8]
  4.8 116.7 %shard_map.130 = (bf16[1024,256]{1,0:T(8,128)(2,1)}, bf16[1024,256]{1,0:T(8,128)(2,1)}, f32[256,256]{1,0:T(8,128)}, f32[1,256]{1,0:T(1,128)}) custom-call(s32[48]{0:T(128)} %take_src.1, s32[48]{0:T(128)} %take_row.1, s32[48]{0:T(128)} %get-tuple-element.12.prev_row, s32[24]{0:T(128)} %get-tuple-element.13.last_row, s32[48]{0:T(128)} %get-tuple-element.14.prev_src, ...), custom_call_target="tpu_custom_call" | custom-call | tf_op jit(solution)/shard_map/pallas_call | solution.py:540
  121.5 0.0 copy-start
  121.5 0.0 copy-start.1
  121.5 1.9 %copy.20 = bf16[1024,256]{1,0:T(8,128)(2,1)} copy(bf16[1024,256]{1,0:T(8,128)(2,1)} %get-tuple-element.24) | data formatting | bytes 1048576
  123.4 1.9 %copy.21 = bf16[1024,256]{1,0:T(8,128)(2,1)} copy(bf16[1024,256]{1,0:T(8,128)(2,1)} %get-tuple-element.25) | data formatting | bytes 1048576
  125.3 0.0 copy-done
  125.3 0.7 copy.22
  126.0 0.0 copy-done.1
  126.0 0.6 copy.23
Async XLA Ops:
  121.5 3.8 %copy-start = (f32[256,256]{1,0:T(8,128)S(1)}, f32[256,256]{1,0:T(8,128)}, u32[]{:S(2)}) copy-start(f32[256,256]{1,0:T(8,128)} %get-tuple-element.26) | copy-start | bytes 786436
  121.5 4.5 %copy-start.1 = (f32[1,256]{1,0:T(1,128)S(1)}, f32[1,256]{1,0:T(1,128)}, u32[]{:S(2)}) copy-start(f32[1,256]{1,0:T(1,128)} %get-tuple-element.19) | copy-start | bytes 3076

commit v3 on v2

--- a/solution.py
+++ b/solution.py
@@ -24,7 +24,6 @@
 def layer_kernel(
     R,
     C,
-    fuse_sum,
     scale,
     take_src,
     take_row,
@@ -53,7 +52,7 @@
         del scratch[:count]
         return taken
 
-    (tiles, cotangent, layer_out, lists) = take(4)
+    (tiles, cotangent, layer_out, lists, features_t) = take(5)
     (list_all, proj, fetch_out, prod, turned, agg, proj_grad) = take(7)
     src = take(H)
     rows_out = take(H)
@@ -64,10 +63,10 @@
     back_out = take(H)
     back_in = take(H)
     (term, bias_acc, bias_row, bias_in1, bias_mid, bias_in2) = take(6)
-    (part_in, part_sum, piece_in, piece_sum, piece_all, part_all) = take(6)
+    (part_in, part_sum, piece_in, piece_sum, piece_all) = take(5)
     (list_s, list_r, fetch_s, fetch_r, rows_s, rows_r) = take(6)
     (slope_s, slope_r, back_s, back_r, b1_s, b1_r, b2_s, b2_r) = take(8)
-    (p1_s, p1_r, p2_s, p2_r, p3_s, p3_r, p4_s, p4_r, local) = take(9)
+    (p1_s, p1_r, p2_s, p2_r, p3_s, p3_r, local) = take(7)
 
     r = lax.axis_index("row")
     c = lax.axis_index("col")
@@ -181,10 +180,12 @@
 
         loop(0, T // group, multiply)
 
-        def chain(k):
-            prod[k] = prod[k] + prod[prev[k]]
-
-        loop(0, T, chain)
+        def chain(g):
+            for u in range(group):
+                k = g * group + u
+                prod[k] = prod[k] + prod[prev[k]]
+
+        loop(0, T // group, chain)
 
     def rows_copy(h, p, frm):
         return col_copy(
@@ -210,6 +211,12 @@
             turned[g * group + u] = tiles[g * group + u].T
 
     loop(0, T // group, turn)
+
+    def turn_features(b):
+        rows = pl.ds(pl.multiple_of(b * side, side), side)
+        features_t[:, rows] = features[rows, :].T
+
+    loop(0, B, turn_features)
 
     strip = 16
 
@@ -289,64 +296,42 @@
         )
 
     F = weight.shape[0]
-    half = F // R
-    piece = half // C
-
-    def part1(h, q, frm):
-        place = pl.ds(pl.multiple_of(q * half, 8), half)
-        return row_copy(
-            term.at[h, place, :], part_in.at[h, frm], p1_s.at[h, q], p1_r.at[h, frm], q
-        )
-
-    def part2(h, p, frm):
+    piece = F // C
+
+    def part1(h, p, frm):
         place = pl.ds(pl.multiple_of(p * piece, 8), piece)
         return col_copy(
-            part_sum.at[h, place, :], piece_in.at[h, frm], p2_s.at[h, p], p2_r.at[h, frm], p
-        )
+            term.at[h, place, :], part_in.at[h, frm], p1_s.at[h, p], p1_r.at[h, frm], p
+        )
+
+    def part2(h, q, frm):
+        return row_copy(part_sum.at[h], piece_in.at[h, frm], p2_s.at[h, q], p2_r.at[h, frm], q)
 
     def part3(h, p, frm):
         return col_copy(piece_sum.at[h], piece_all.at[h, frm], p3_s.at[h, p], p3_r.at[h, frm], p)
 
-    def part4(h, q, frm):
-        return row_copy(piece_all.at[h], part_all.at[h, frm], p4_s.at[h, q], p4_r.at[h, frm], q)
-
     def sum1(h):
-        if fuse_sum:
-            row_peers(lambda q: part1(h, q, r).start())
-            part_in[h, r] = term[h, pl.ds(pl.multiple_of(r * half, 8), half), :]
+        col_peers(lambda p: part1(h, p, c).start())
+        part_in[h, c] = term[h, pl.ds(pl.multiple_of(c * piece, 8), piece), :]
 
     def sum2(h):
-        if fuse_sum:
-            row_peers(lambda q: part1(h, q, q).wait_recv())
-            part_sum[h] = jnp.sum(part_in[h], axis=0)
-            col_peers(lambda p: part2(h, p, c).start())
-            piece_in[h, c] = part_sum[h, pl.ds(pl.multiple_of(c * piece, 8), piece), :]
+        col_peers(lambda p: part1(h, p, p).wait_recv())
+        part_sum[h] = jnp.sum(part_in[h], axis=0)
+        row_peers(lambda q: part2(h, q, r).start())
+        piece_in[h, r] = part_sum[h]
 
     def sum3(h):
-        if fuse_sum:
-            col_peers(lambda p: part2(h, p, p).wait_recv())
-            piece_sum[h] = jnp.sum(piece_in[h], axis=0) * scale
-            col_peers(lambda p: part3(h, p, c).start())
-            piece_all[h, c] = piece_sum[h]
+        row_peers(lambda q: part2(h, q, q).wait_recv())
+        piece_sum[h] = jnp.sum(piece_in[h], axis=0) * scale
+        col_peers(lambda p: part3(h, p, c).start())
+        piece_all[h, c] = piece_sum[h]
 
     def sum4(h):
-        if fuse_sum:
-            col_peers(lambda p: part3(h, p, p).wait_recv())
-            row_peers(lambda q: part4(h, q, r).start())
-            part_all[h, r] = piece_all[h]
-
-    def sum5(h):
-        cols = slice(h * FC, (h + 1) * FC)
-        if fuse_sum:
-            row_peers(lambda q: part4(h, q, q).wait_recv())
-            grad_weight[:, cols] = part_all[h].reshape(F, FC)
-        else:
-            grad_weight[:, cols] = term[h]
+        col_peers(lambda p: part3(h, p, p).wait_recv())
+        grad_weight[:, h * FC : (h + 1) * FC] = piece_all[h].reshape(F, FC)
 
     def source_part(h):
         col_peers(lambda p: slope_copy(h, p, p).wait_recv())
-        if h > 0:
-            sum2(h - 1)
         tile_sums(turned, row_vals[h], take_row, CO, prev_src)
 
         def send_back(q):
@@ -372,12 +357,7 @@
             proj_grad[rows, cols] = total.astype(BF16)
 
         loop(0, B, gather_back)
-        term[h] = lax.dot_general(
-            features[...],
-            proj_grad[:, cols],
-            (((0,), (0,)), ((), ())),
-            preferred_element_type=F32,
-        )
+        term[h] = jnp.dot(features_t[...], proj_grad[:, cols], preferred_element_type=F32)
         sum1(h)
 
     for h in range(H):
@@ -387,11 +367,9 @@
             bias_mid[...] = jnp.sum(bias_in1[...], axis=0)
             col_peers(lambda p: bias2(p, c).start())
             bias_in2[c] = bias_mid[...]
-        else:
-            sum3(h - 1)
         weight_part(h)
         if h > 0:
-            sum4(h - 1)
+            sum2(h - 1)
 
     def features_back(b):
         rows = pl.ds(pl.multiple_of(b * side, side), side)
@@ -401,21 +379,18 @@
 
     last = H - 1
     loop(0, B // 2, features_back)
+    for h in range(last):
+        sum3(h)
     sum2(last)
     loop(B // 2, B, features_back)
     col_peers(lambda p: bias2(p, p).wait_recv())
     grad_bias[...] = jnp.sum(jnp.sum(bias_in2[...], axis=0), axis=0, keepdims=True) * scale
     sum3(last)
-    for h in range(last):
-        sum5(h)
-    sum4(last)
-    sum5(last)
-    if fuse_sum:
-        for h in range(H):
-            row_peers(lambda q, h=h: part1(h, q, r).wait_send())
-            col_peers(lambda p, h=h: part2(h, p, c).wait_send())
-            col_peers(lambda p, h=h: part3(h, p, c).wait_send())
-            row_peers(lambda q, h=h: part4(h, q, r).wait_send())
+    for h in range(H):
+        sum4(h)
+        col_peers(lambda p, h=h: part1(h, p, c).wait_send())
+        row_peers(lambda q, h=h: part2(h, q, r).wait_send())
+        col_peers(lambda p, h=h: part3(h, p, c).wait_send())
     out_copy.wait()
 
     row_peers(
@@ -473,9 +448,7 @@
     CF = fetch_list.shape[1]
     CO = deliver_list.shape[1]
     FC = F // H
-    half = F // R
-    piece = half // C
-    fuse_sum = F % R == 0 and half % C == 0 and piece % 8 == 0
+    piece = F // C
     scale = 1.0 / math.sqrt(N * R * C)
     list_rows = -(-CF // 8) * 8
     vmem = pl.BlockSpec(memory_space=pltpu.VMEM)
@@ -491,12 +464,12 @@
     )(tile_source, tile_target, tile_count)
     V = pltpu.VMEM
     dma = pltpu.SemaphoreType.DMA
-    small = piece if fuse_sum else 8
     scratch = [
         V((T, side, side), BF16),
         V((N, F), BF16),
         V((N, F), BF16),
         V((R, list_rows, F), jnp.int32),
+        V((F, N), BF16),
         V((R, list_rows, F), jnp.int32),
         V((H, B, side, FC), BF16),
         V((H, R, CF, side, FC), BF16),
@@ -518,12 +491,11 @@
         V((R, 8, F), F32),
         V((8, F), F32),
         V((C, 8, F), F32),
-        V((H, R, half, FC), F32),
-        V((H, half, FC), F32),
-        V((H, C, small, FC), F32),
-        V((H, small, FC), F32),
-        V((H, C, small, FC), F32),
-        V((H, R, C, small, FC), F32),
+        V((H, C, piece, FC), F32),
+        V((H, piece, FC), F32),
+        V((H, R, piece, FC), F32),
+        V((H, piece, FC), F32),
+        V((H, C, piece, FC), F32),
         *[dma((R,))] * 2,
         *[dma((H, R))] * 2,
         *[dma((H, C))] * 2,
@@ -531,14 +503,13 @@
         *[dma((H, R))] * 2,
         *[dma((R,))] * 2,
         *[dma((C,))] * 2,
+        *[dma((H, C))] * 2,
         *[dma((H, R))] * 2,
         *[dma((H, C))] * 2,
-        *[dma((H, C))] * 2,
-        *[dma((H, R))] * 2,
         dma((3,)),
     ]
     layer_out, grad_features, grad_weight, grad_bias = pl.pallas_call(
-        functools.partial(layer_kernel, R, C, fuse_sum, scale),
+        functools.partial(layer_kernel, R, C, scale),
         out_shape=(
             jax.ShapeDtypeStruct((N, F), BF16),
             jax.ShapeDtypeStruct((N, F), BF16),
@@ -567,8 +538,6 @@
         cotangent,
     )
     grad_bias = grad_bias.reshape(F)
-    if not fuse_sum:
-        grad_weight = lax.psum(grad_weight, ("row", "col")) * scale
     return (layer_out, grad_features, grad_weight, grad_bias)
 
 

time: 127 us -> 122 us (0.961)
  Pallas kernels: 119 us -> 114 us
    pallas_call x1, Pallas kernels: 117 us -> 112 us  [body(): pl.pallas_call(functools.partial(layer_kernel, R, C, scale), out_shape=(j...]
where the time goes in v3:
time: 122 us
  Pallas kernels  114 us (93%)
  local copies, waits for them, and re-layouts  6.4 us (5%)
  between operations  1.31 us (1%)
    pallas_call x1, Pallas kernels, body(): pl.pallas_call(functools.partial(layer_kernel, R, C, scale), out_shape=(j...  112 us
    unnamed x9, local copies, waits for them, and re-layouts  6.4 us

profile of v3, /device:TPU:0, one launch (start us, length us, event | category | flops | bytes accessed | tf_op | source)
XLA Modules:
  0.0 121.7 jit_solution(10555690924542391230)
XLA Ops:
  1.3 2.1 %shard_map.129 = (s32[48]{0:T(128)}, s32[24]{0:T(128)}, s32[48]{0:T(128)}, s32[12]{0:T(128)}) custom-call(s32[48]{0:T(128)} %take_src.1, s32[48]{0:T(128)} %take_row.1, s32[1]{0:T(128)S(6)} %copy.19.count), custom_call_target="tpu_custom_call" | custom-call | tf_op jit(solution)/shard_map/pallas_call | solution.py:457
  3.4 1.4 %copy.14.deliver = s32[8,3]{1,0:T(8,128)} copy(s32[8,3]{0,1:T(4,128)} %param.18) | data formatting | bytes 192 | tf_op args[8]
  4.8 111.8 %shard_map.130 = (bf16[1024,256]{1,0:T(8,128)(2,1)}, bf16[1024,256]{1,0:T(8,128)(2,1)}, f32[256,256]{1,0:T(8,128)}, f32[1,256]{1,0:T(1,128)}) custom-call(s32[48]{0:T(128)} %take_src.1, s32[48]{0:T(128)} %take_row.1, s32[48]{0:T(128)} %get-tuple-element.12.prev_row, s32[24]{0:T(128)} %get-tuple-element.13.last_row, s32[48]{0:T(128)} %get-tuple-element.14.prev_src, ...), custom_call_target="tpu_custom_call" | custom-call | tf_op jit(solution)/shard_map/pallas_call | solution.py:511
  116.6 0.0 copy-start
  116.6 0.0 copy-start.1
  116.6 1.9 %copy.20 = bf16[1024,256]{1,0:T(8,128)(2,1)} copy(bf16[1024,256]{1,0:T(8,128)(2,1)} %get-tuple-element.24) | data formatting | bytes 1048576
  118.5 1.9 %copy.21 = bf16[1024,256]{1,0:T(8,128)(2,1)} copy(bf16[1024,256]{1,0:T(8,128)(2,1)} %get-tuple-element.25) | data formatting | bytes 1048576
  120.4 0.0 copy-done
  120.4 0.7 copy.22
  121.1 0.0 copy-done.1
  121.1 0.6 copy.23
Async XLA Ops:
  116.6 3.8 %copy-start = (f32[256,256]{1,0:T(8,128)S(1)}, f32[256,256]{1,0:T(8,128)}, u32[]{:S(2)}) copy-start(f32[256,256]{1,0:T(8,128)} %get-tuple-element.26) | copy-start | bytes 786436
  116.6 4.5 %copy-start.1 = (f32[1,256]{1,0:T(1,128)S(1)}, f32[1,256]{1,0:T(1,128)}, u32[]{:S(2)}) copy-start(f32[1,256]{1,0:T(1,128)} %get-tuple-element.19) | copy-start | bytes 3076
